TPU v7x, 32 devices: a whole 2x2x4 slice. The times are simulated.
32 devices in a mesh: head: 4 (over x, core), seq: 8 (over z, y).
Axes of the slice: x: 2, y: 2, z: 4, core: 2. Of those that a mesh axis runs over, the one named last changes fastest.
Arguments:
- x_input: bfloat16 [8192, 16384], P('seq', 'head'), may hold values from -5 to 5
- bc_input: bfloat16 [2, 8192, 1024], P(None, 'seq', 'head'), may hold values from -5 to 5
- dt_input: bfloat16 [8192, 128], P('seq', 'head'), may hold values from -8 to 256
- z_gate: bfloat16 [8192, 16384], P('seq', 'head'), may hold values from -400 to 400
- conv_x: float32 [4, 16384], P(None, 'head'), may hold values from -2 to 2
- conv_bc: float32 [2, 4, 1024], P(None, None, 'head'), may hold values from -2 to 2
- dt_bias: float32 [128], P('head'), may hold values from -0.3 to 0.3
- a_log: float32 [128], P('head'), may hold values from -10 to 1
- d_skip: float32 [128], P('head'), may hold values from 0.5 to 1.5
- init_state: float32 [128, 128, 128], P('head'), may hold values from -5 to 5
- norm_gain: float32 [16384], P('head'), may hold values from 0.5 to 1.5
Outputs:
- normed: bfloat16 [8192, 16384], P('seq', 'head')
All inputs are finite; a program needn't handle non-finite values.
Results may differ from a plain program's by a relative error of at most 0.0034.
Values may be sent and summed in bfloat16 or wider, within the bound.
A program may use at most 128 MiB of HBM per device.

v0:
```python
import jax
import jax.numpy as jnp
from jax import lax
from jax.sharding import PartitionSpec as P

SPAN = 256
INNER = 16384
norm_eps = 1e-05


def from_behind(value, axis, by):
    length = lax.axis_size(axis)
    pairs = [(i, i + by) for i in range(length) if 0 <= i + by < length]
    return lax.ppermute(value, axis, pairs)


def combine_states(earlier, later):
    return (earlier[0] * later[0], later[0][..., None, None] * earlier[1] + later[1])


def prefix_sources(pieces):
    inclusive = lax.associative_scan(combine_states, pieces, axis=0)
    return jnp.concatenate([jnp.zeros_like(pieces[1][:1]), inclusive[1][:-1]], axis=0)


def local(
    x_input,
    bc_input,
    dt_input,
    z_gate,
    conv_x,
    conv_bc,
    dt_bias,
    a_log,
    d_skip,
    init_state,
    norm_gain,
):
    row_count = x_input.shape[0]
    channels = x_input.shape[1]
    heads_here = a_log.shape[0]
    head_dim = init_state.shape[1]
    state_dim = init_state.shape[2]
    groups_here = bc_input.shape[2] // state_dim
    group_heads = heads_here // groups_here
    segment_len = SPAN
    segments = row_count // segment_len
    rim_rows = conv_x.shape[0] - 1
    x_rim, bc_rim = from_behind(
        (x_input[row_count - rim_rows :], bc_input[:, row_count - rim_rows :]), "seq", 1
    )
    x_full = jnp.concatenate([x_rim, x_input], axis=0)
    bc_full = jnp.concatenate([bc_rim, bc_input], axis=1)
    x_sum = jnp.zeros((row_count, channels), jnp.float32)
    bc_sum = jnp.zeros(bc_input.shape, jnp.float32)
    for tap_index in range(rim_rows + 1):
        x_sum = x_sum + conv_x[tap_index] * x_full[tap_index : tap_index + row_count]
        bc_sum = (
            bc_sum
            + conv_bc[:, tap_index][:, None, :] * bc_full[:, tap_index : tap_index + row_count]
        )
    x_conv = jax.nn.silu(x_sum).astype(jnp.bfloat16)
    bc_conv = jax.nn.silu(bc_sum).astype(jnp.bfloat16)
    b_mat = bc_conv[0].reshape(segments, segment_len, groups_here, state_dim)
    c_mat = bc_conv[1].reshape(segments, segment_len, groups_here, state_dim)
    time_step = jax.nn.softplus(dt_input.astype(jnp.float32) + dt_bias).reshape(
        segments, segment_len, heads_here
    )
    log_cum = jnp.cumsum(-jnp.exp(a_log) * time_step, axis=1)
    scores = jnp.einsum("clgn,csgn->cgls", c_mat, b_mat, preferred_element_type=jnp.float32)
    cum_heads = jnp.transpose(log_cum, (0, 2, 1))
    step_heads = jnp.transpose(time_step, (0, 2, 1))
    log_gap = cum_heads[:, :, :, None] - cum_heads[:, :, None, :]
    causal = jnp.arange(segment_len)[:, None] >= jnp.arange(segment_len)[None, :]
    weights = (
        jnp.where(causal, jnp.exp(jnp.where(causal, log_gap, 0.0)), 0.0) * step_heads[:, :, None, :]
    )
    mixing = (
        scores[:, :, None]
        * weights.reshape(segments, groups_here, group_heads, segment_len, segment_len)
    ).astype(jnp.bfloat16)
    x_heads = x_conv.reshape(segments, segment_len, groups_here, group_heads, head_dim)
    local_part = jnp.einsum(
        "cghls,csghp->clghp", mixing, x_heads, preferred_element_type=jnp.float32
    )
    tail_weight = jnp.exp(log_cum[:, -1:, :] - log_cum) * time_step
    x_weighted = (
        x_heads * tail_weight.reshape(segments, segment_len, groups_here, group_heads, 1)
    ).astype(jnp.bfloat16)
    block_state = jnp.einsum(
        "clghp,clgn->cghpn", x_weighted, b_mat, preferred_element_type=jnp.float32
    )
    block_decay = jnp.exp(log_cum[:, -1, :]).reshape(segments, groups_here, group_heads)
    running = jnp.zeros((groups_here, group_heads, head_dim, state_dim), jnp.float32)
    factor = jnp.ones((groups_here, group_heads), jnp.float32)
    starts = []
    factors = []
    for piece_index in range(segments):
        starts.append(running)
        factors.append(factor)
        running = block_decay[piece_index][..., None, None] * running + block_state[piece_index]
        factor = factor * block_decay[piece_index]
    is_first = lax.axis_index("seq") == 0
    seed_state = init_state.reshape(groups_here, group_heads, head_dim, state_dim)
    summary = running + jnp.where(is_first, factor[..., None, None] * seed_state, 0.0)
    source_count = lax.axis_size("seq")
    per_piece = heads_here // source_count
    flat_states = summary.reshape(source_count, per_piece, head_dim, state_dim)
    piece_decays = factor.reshape(source_count, per_piece)
    ordered = prefix_sources(
        (
            lax.all_to_all(piece_decays, "seq", split_axis=0, concat_axis=0, tiled=True),
            lax.all_to_all(flat_states, "seq", split_axis=0, concat_axis=0, tiled=True),
        )
    )
    prefix = lax.all_to_all(ordered, "seq", split_axis=0, concat_axis=0, tiled=True).reshape(
        groups_here, group_heads, head_dim, state_dim
    )
    incoming = prefix + jnp.where(is_first, seed_state, 0.0)
    start_states = jnp.stack(starts) + jnp.stack(factors)[..., None, None] * incoming
    state_low = start_states.astype(jnp.bfloat16)
    carried_part = jnp.exp(log_cum).reshape(
        segments, segment_len, groups_here, group_heads, 1
    ) * jnp.einsum("clgn,cghpn->clghp", c_mat, state_low, preferred_element_type=jnp.float32)
    skip_part = d_skip.reshape(groups_here, group_heads, 1) * x_heads
    mixed_out = (local_part + carried_part + skip_part).reshape(row_count, channels)
    gated_out = mixed_out * jax.nn.silu(z_gate.astype(jnp.float32))
    square_sum = jnp.sum(gated_out * gated_out, axis=1)
    total_square = lax.psum(square_sum, "head")
    inverse_rms = lax.rsqrt(total_square / INNER + norm_eps)
    return (gated_out * inverse_rms[:, None] * norm_gain).astype(jnp.bfloat16)


def solution(mesh):
    placed = (
        P("seq", "head"),
        P(None, "seq", "head"),
        P("seq", "head"),
        P("seq", "head"),
        P(None, "head"),
        P(None, None, "head"),
        P("head"),
        P("head"),
        P("head"),
        P("head", None, None),
        P("head"),
    )
    return jax.shard_map(
        local, mesh=mesh, in_specs=placed, out_specs=P("seq", "head"), check_vma=False
    )
```

profile of v0, /device:TPU:0, one launch (start us, length us, event | category | flops | bytes accessed | tf_op | source)
XLA Modules:
  0.0 324.5 jit_solution(15686120314785858558)
XLA Ops:
  0.7 4.9 %collective-permute-start.1 = (bf16[2,3,256]{2,1,0:T(4,128)(2,1)S(1)}, bf16[2,3,256]{2,1,0:T(4,128)(2,1)S(1)}, u32[]{:S(2)}, u32[]{:S(2)}) collective-permute-start(bf16[2,3,256]{2,1,0:T(4,128)(2,1)S(1)} %slice.173), channel_id=1, source_target_pairs={{0,1},{1,2},{2,3},{3,4},{4,5},{5,6},{6,7},{8,9},{9,10},{10,11},{11... | collective-permute-start | bytes 9224 | tf_op jit(solution)/shard_map/ppermute | solution.py:14
  6.4 3.4 %collective-permute-start = (bf16[3,4096]{1,0:T(4,128)(2,1)S(1)}, bf16[3,4096]{1,0:T(4,128)(2,1)S(1)}, u32[]{:S(2)}, u32[]{:S(2)}) collective-permute-start(bf16[3,4096]{1,0:T(4,128)(2,1)S(1)} %slice.165), channel_id=1, source_target_pairs={{0,1},{1,2},{2,3},{3,4},{4,5},{5,6},{6,7},{8,9},{9,10},{10,11},{11... | collective-permute-start | bytes 73736 | tf_op jit(solution)/shard_map/ppermute | solution.py:14
  11.9 2.3 reduce-window.6
  15.9 4.8 %all-to-all-start.1 = ((f32[8,1,4]{2,1,0:T(1,128)}), f32[8,1,4]{2,1,0:T(1,128)}, u32[]{:S(2)}, u32[]{:S(2)}) async-start(f32[8,1,4]{2,1,0:T(1,128)} %bitcast.18), calls=%async_computation.1 | async-start | bytes 8192 | tf_op jit(solution)/shard_map/all_to_all | solution.py:112
  26.3 3.5 %multiply_convert_fusion.6 = bf16[2,1024,256]{2,1,0:T(8,128)(2,1)S(1)} fusion(bf16[2,1024,256]{2,1,0:T(8,128)(2,1)} %param.12, bf16[2,3,256]{2,1,0:T(4,128)(2,1)S(1)} %collective-permute-done.1, f32[2,256]{1,0:T(2,128)S(1)} %get-tuple-element.41, f32[2,256]{1,0:T(2,128)S(1)} %get-tuple-element.42, f32[2,256]{1,0:T(2,128)S(1)} %get-tuple-element.43, ...), kind=kLoop, calls=%fused_computation.41 | loop fusion | flops 13107200 | bytes 2108416 | tf_op jit(solution)/shard_map/convert_element_type | solution.py:63
  30.8 18.9 %fusion.20 = bf16[128,8,32,128]{3,1,2,0:T(8,128)(2,1)} fusion(bf16[1024,4096]{1,0:T(8,128)(2,1)} %param.11, f32[4096]{0:T(1024)S(1)} %bitcast.98, bf16[3,4096]{1,0:T(4,128)(2,1)S(1)} %collective-permute-done, f32[4096]{0:T(1024)S(1)} %bitcast.99, f32[4096]{0:T(1024)S(1)} %bitcast.97, f32[4096]{0:T(1024)S(1)} %bitcast.96), kind=kLoop, calls=%fused_computation.32 | loop fusion | flops 104857600 | bytes 16867328
  49.8 9.4 %copy.115 = bf16[128,8,32,128]{3,2,1,0:T(8,128)(2,1)} copy(bf16[128,8,32,128]{3,1,2,0:T(8,128)(2,1)} %fusion.20) | data formatting | bytes 16777216
  59.2 13.7 %copy.89 = bf16[4,256,2,16,128]{1,4,3,2,0:T(8,128)(2,1)} copy(bf16[4,256,2,16,128]{4,3,2,1,0:T(8,128)(2,1)} %bitcast.83) | data formatting | bytes 16777216 | tf_op jit(solution)/shard_map/reshape | solution.py:82
  72.9 5.7 %fusion.16 = f32[4,2,16,128,128]{4,3,2,1,0:T(8,128)S(1)} fusion(bf16[4,256,2,16,128]{1,4,3,2,0:T(8,128)(2,1)} %copy.89, f32[4,256,2,16]{1,3,2,0:T(8,128)S(1)} %bitcast.94, bf16[4,256,2,128,1]{3,2,1,0,4:T(2,128)(2,1)S(1)} %bitcast.91), kind=kOutput, calls=%fused_computation.27 | convolution fusion | flops 1086324736 | bytes 17432576 | tf_op jit(solution)/shard_map/clghp,clgn->cghpn/dot_general | solution.py:90
  78.7 6.3 %multiply_add_fusion = (f32[1,2,16,128,128]{4,3,2,1,0:T(8,128)}, f32[1,2,16,128,128]{4,3,2,1,0:T(8,128)}, f32[1,2,16,128,128]{4,3,2,1,0:T(8,128)}, f32[1,2,16,12...) fusion(f32[2,16]{1,0:T(2,128)S(1)} %copy-done.13, ...), kind=kLoop, calls=%fused_computation.39 | loop fusion | flops 2621440 | bytes 23069056 | tf_op jit(solution)/shard_map/add | solution.py:101
  85.0 6.2 %select_add_fusion = f32[8,4,128,128]{3,2,1,0:T(8,128)} fusion(f32[8,4,128,128]{3,2,1,0:T(8,128)} %bitcast.89, f32[8,4,128,128]{3,2,1,0:T(8,128)} %bitcast.88, f32[8,4,128,128]{3,2,1,0:T(8,128)} %bitcast.87, f32[8,4,128,128]{3,2,1,0:T(8,128)} %bitcast.86, f32[8,4,128,128]{3,2,1,0:T(8,128)} %bitcast.85, f32[8,4]{1,0:T(8,128)S(1)} %copy-done.6, ...), kind=kLoop, calls=%fused_computation.38 | loop fusion | flops 5242880 | bytes 12583553 | tf_op jit(solution)/shard_map/add | solution.py:105
  91.3 6.0 %all-to-all-start = ((f32[8,4,128,128]{3,2,1,0:T(8,128)}), f32[8,4,128,128]{3,2,1,0:T(8,128)S(1)}, u32[]{:S(2)}, u32[]{:S(2)}) async-start(f32[8,4,128,128]{3,2,1,0:T(8,128)} %select_add_fusion), calls=%async_computation | async-start | bytes 4194304 | tf_op jit(solution)/shard_map/all_to_all | solution.py:113
  99.1 45.2 %all-to-all-done = f32[8,4,128,128]{3,2,1,0:T(8,128)S(1)} async-done(((f32[8,4,128,128]{3,2,1,0:T(8,128)}), f32[8,4,128,128]{3,2,1,0:T(8,128)S(1)}, u32[]{:S(2)}, u32[]{:S(2)}) %all-to-all-start) | async-done | bytes 2097184 | tf_op jit(solution)/shard_map/all_to_all | solution.py:113
  146.5 3.5 %pad.22 = f32[4,4,128,128]{3,2,1,0:T(8,128)S(1)} pad(f32[2,4,128,128]{3,2,1,0:T(8,128)} %pad_maximum_fusion.3, f32[]{:T(128)} %constant.9.clone.1), padding=0_1_1x0_0_0x0_0_0x0_0_0 | pad | bytes 1572868 | tf_op jit(solution)/shard_map/pad | solution.py:22
  150.0 5.7 %pad.23 = f32[4,4,128,128]{3,2,1,0:T(8,128)} pad(f32[2,4,128,128]{3,2,1,0:T(8,128)} %pad_add_fusion, f32[]{:T(128)} %constant.9.clone.1), padding=1_0_1x0_0_0x0_0_0x0_0_0 | pad | bytes 1572868 | tf_op jit(solution)/shard_map/pad | solution.py:22
  155.7 2.3 add.159
  158.1 10.1 %pad.114 = f32[8,4,128,128]{3,2,1,0:T(8,128)} pad(f32[4,4,128,128]{3,2,1,0:T(8,128)} %add.159, f32[]{:T(128)} %constant.9.clone.1), padding=1_0_1x0_0_0x0_0_0x0_0_0 | pad | bytes 3145732
  168.2 1.3 fusion.28
  169.9 1.7 slice_add_fusion.3
  171.6 1.6 concatenate.19
  173.2 4.4 %all-to-all-start.2 = ((f32[8,4,128,128]{3,2,1,0:T(8,128)}), f32[8,4,128,128]{3,2,1,0:T(8,128)}, u32[]{:S(2)}, u32[]{:S(2)}) async-start(f32[8,4,128,128]{3,2,1,0:T(8,128)} %concatenate.19), calls=%async_computation.2 | async-start | bytes 4194304 | tf_op jit(solution)/shard_map/all_to_all | solution.py:116
  179.1 3.1 broadcast_select_fusion
  183.4 1.8 fusion.31
  185.2 40.2 %all-to-all-done.2 = f32[8,4,128,128]{3,2,1,0:T(8,128)} async-done(((f32[8,4,128,128]{3,2,1,0:T(8,128)}), f32[8,4,128,128]{3,2,1,0:T(8,128)}, u32[]{:S(2)}, u32[]{:S(2)}) %all-to-all-start.2) | async-done | bytes 2097184 | tf_op jit(solution)/shard_map/all_to_all | solution.py:116
  225.4 2.6 bitcast_add_fusion
  228.1 10.5 %fusion.21 = f32[4,2,16,128,256]{4,3,2,1,0:T(8,128)} fusion(f32[1,2,16,128,128]{4,3,2,1,0:T(8,128)S(1)} %copy-done, f32[1,2,16,128,128]{4,3,2,1,0:T(8,128)} %get-tuple-element.14, f32[1,2,16,128,128]{4,3,2,1,0:T(8,128)} %get-tuple-element.15, f32[4]{0:T(128)S(1)} %pad.35.clone, f32[2,16,128,128]{3,2,1,0:T(8,128)S(1)} %bitcast_add_fusion, ...), kind=kOutput, calls=%fused_computation.33 | convolution fusion | flops 1086324736 | bytes 25690640 | tf_op jit(solution)/shard_map/clgn,cghpn->clghp/dot_general | solution.py:124
  238.6 17.5 %fusion.2 = f32[4,256,2,16,128]{1,4,3,2,0:T(8,128)} fusion(bf16[4,256,2,16,128]{1,4,3,2,0:T(8,128)(2,1)S(1)} %bitcast.82, f32[4,2,16,128,256]{4,3,2,1,0:T(8,128)} %fusion.21, f32[4,2,16,256]{3,2,1,0:T(8,128)S(1)} %copy.88, f32[4,2,16,256]{3,2,1,0:T(8,128)S(1)} %reduce_window_sum.27, f32[4,2,256,256]{3,2,1,0:T(8,128)} %fusion.31, ...), kind=kOutput, calls=%fused_computation.7 | convolution fusion | flops 2218786816 | bytes 44499072 | tf_op jit(solution)/shard_map/cghls,csghp->clghp/dot_general | solution.py:83
  256.1 19.9 %copy.100 = f32[4,256,2,16,128]{4,3,2,1,0:T(8,128)} copy(f32[4,256,2,16,128]{1,4,3,2,0:T(8,128)} %fusion.2) | data formatting | bytes 33554432 | tf_op jit(solution)/shard_map/add | solution.py:126
  276.0 18.2 %reshape.230 = f32[1024,4096]{1,0:T(8,128)} reshape(f32[4,256,2,16,128]{4,3,2,1,0:T(8,128)} %copy.100) | data formatting | bytes 33554432 | tf_op jit(solution)/shard_map/reshape | solution.py:126
  294.2 10.7 %multiply_reduce_fusion = f32[1024]{0:T(1024)S(1)} fusion(f32[1024,4096]{1,0:T(8,128)} %reshape.230, bf16[1024,4096]{1,0:T(8,128)(2,1)} %param.14), kind=kLoop, calls=%fused_computation.15 | loop fusion | flops 33553408 | bytes 25169920 | tf_op jit(solution)/shard_map/reduce_sum | solution.py:128
  304.9 5.7 %psum.7 = f32[1024]{0:T(1024)S(1)} all-reduce(f32[1024]{0:T(1024)S(1)} %multiply_reduce_fusion), channel_id=1, replica_groups=mesh['head'=4,'seq'=8] {'head'}, use_global_device_ids=true, to_apply=%region_3.4 | all-reduce | flops 1024 | bytes 8192 | tf_op jit(solution)/shard_map/psum | solution.py:129
  310.6 13.9 %multiply_convert_fusion.2 = bf16[1024,4096]{1,0:T(8,128)(2,1)} fusion(f32[4096]{0:T(1024)S(1)} %copy-done.5, f32[1024]{0:T(1024)S(1)} %add_rsqrt_fusion, f32[1024,4096]{1,0:T(8,128)} %reshape.230, bf16[1024,4096]{1,0:T(8,128)(2,1)} %param.14), kind=kLoop, calls=%fused_computation.14 | loop fusion | flops 37748736 | bytes 33574912 | tf_op jit(solution)/shard_map/convert_element_type | solution.py:131
  (110 shorter events, 18.8 us)
Async XLA Ops:
  0.7 25.6 %collective-permute-start.1 = (bf16[2,3,256]{2,1,0:T(4,128)(2,1)S(1)}, bf16[2,3,256]{2,1,0:T(4,128)(2,1)S(1)}, u32[]{:S(2)}, u32[]{:S(2)}) collective-permute-start(bf16[2,3,256]{2,1,0:T(4,128)(2,1)S(1)} %slice.173), channel_id=1, source_target_pairs={{0,1},{1,2},{2,3},{3,4},{4,5},{5,6},{6,7},{8,9},{9,10},{10,11},{11... | collective-permute-start | bytes 9224 | tf_op jit(solution)/shard_map/ppermute | solution.py:14
  6.4 24.4 %collective-permute-start = (bf16[3,4096]{1,0:T(4,128)(2,1)S(1)}, bf16[3,4096]{1,0:T(4,128)(2,1)S(1)}, u32[]{:S(2)}, u32[]{:S(2)}) collective-permute-start(bf16[3,4096]{1,0:T(4,128)(2,1)S(1)} %slice.165), channel_id=1, source_target_pairs={{0,1},{1,2},{2,3},{3,4},{4,5},{5,6},{6,7},{8,9},{9,10},{10,11},{11... | collective-permute-start | bytes 73736 | tf_op jit(solution)/shard_map/ppermute | solution.py:14
  15.3 8.5 %copy-start.7 = (f32[32]{0:T(128)}, f32[32]{0:T(128)S(1)}, u32[]{:S(2)}) copy-start(f32[32]{0:T(128)S(1)} %get-tuple-element.40) | copy-start | bytes 388
  15.3 8.5 %copy-start.9 = (f32[32]{0:T(128)}, f32[32]{0:T(128)S(1)}, u32[]{:S(2)}) copy-start(f32[32]{0:T(128)S(1)} %get-tuple-element.38) | copy-start | bytes 388
  15.9 75.3 %all-to-all-start.1 = ((f32[8,1,4]{2,1,0:T(1,128)}), f32[8,1,4]{2,1,0:T(1,128)}, u32[]{:S(2)}, u32[]{:S(2)}) async-start(f32[8,1,4]{2,1,0:T(1,128)} %bitcast.18), calls=%async_computation.1 | async-start | bytes 8192 | tf_op jit(solution)/shard_map/all_to_all | solution.py:112
  30.8 42.1 %copy-start.1 = (bf16[4,256,2,128]{3,2,1,0:T(2,128)(2,1)}, bf16[4,256,2,128]{3,2,1,0:T(2,128)(2,1)S(1)}, u32[]{:S(2)}) copy-start(bf16[4,256,2,128]{3,2,1,0:T(2,128)(2,1)S(1)} %reshape_squeeze.7) | copy-start | bytes 1572868
  72.9 5.8 %copy-start.11 = (f32[2,16]{1,0:T(2,128)S(1)}, f32[2,16]{1,0:T(2,128)}, u32[]{:S(2)}) copy-start(f32[2,16]{1,0:T(2,128)} %mul.426) | copy-start | bytes 388
  72.9 5.8 %copy-start.12 = (f32[2,16]{1,0:T(2,128)S(1)}, f32[2,16]{1,0:T(2,128)}, u32[]{:S(2)}) copy-start(f32[2,16]{1,0:T(2,128)} %mul.432) | copy-start | bytes 388
  72.9 5.8 %copy-start.13 = (f32[2,16]{1,0:T(2,128)S(1)}, f32[2,16]{1,0:T(2,128)}, u32[]{:S(2)}) copy-start(f32[2,16]{1,0:T(2,128)} %mul.435) | copy-start | bytes 388
  78.7 6.4 %copy-start.6 = (f32[8,4]{1,0:T(8,128)S(1)}, f32[8,4]{1,0:T(8,128)}, u32[]{:S(2)}) copy-start(f32[8,4]{1,0:T(8,128)} %get-tuple-element.37) | copy-start | bytes 388
  91.3 53.1 %all-to-all-start = ((f32[8,4,128,128]{3,2,1,0:T(8,128)}), f32[8,4,128,128]{3,2,1,0:T(8,128)S(1)}, u32[]{:S(2)}, u32[]{:S(2)}) async-start(f32[8,4,128,128]{3,2,1,0:T(8,128)} %select_add_fusion), calls=%async_computation | async-start | bytes 4194304 | tf_op jit(solution)/shard_map/all_to_all | solution.py:113
  169.6 8.0 %copy-start.10 = (f32[32]{0:T(128)S(1)}, f32[32]{0:T(128)}, u32[]{:S(2)}) copy-start(f32[32]{0:T(128)} %copy-done.9) | copy-start | bytes 388
  169.6 8.1 %copy-start.8 = (f32[32]{0:T(128)S(1)}, f32[32]{0:T(128)}, u32[]{:S(2)}) copy-start(f32[32]{0:T(128)} %copy-done.7) | copy-start | bytes 388
  169.6 8.2 %copy-start.14 = (f32[32]{0:T(128)S(1)}, f32[32]{0:T(128)}, u32[]{:S(2)}) copy-start(f32[32]{0:T(128)} %get-tuple-element.5) | copy-start | bytes 388
  169.6 8.7 %copy-start.15 = (f32[32]{0:T(128)S(1)}, f32[32]{0:T(128)}, u32[]{:S(2)}) copy-start(f32[32]{0:T(128)} %param.19) | copy-start | bytes 388
  171.6 11.8 %copy-start.2 = (bf16[4,256,2,128]{3,2,1,0:T(2,128)(2,1)S(1)}, bf16[4,256,2,128]{3,2,1,0:T(2,128)(2,1)}, u32[]{:S(2)}) copy-start(bf16[4,256,2,128]{3,2,1,0:T(2,128)(2,1)} %copy-done.1) | copy-start | bytes 1572868
  173.2 52.2 %all-to-all-start.2 = ((f32[8,4,128,128]{3,2,1,0:T(8,128)}), f32[8,4,128,128]{3,2,1,0:T(8,128)}, u32[]{:S(2)}, u32[]{:S(2)}) async-start(f32[8,4,128,128]{3,2,1,0:T(8,128)} %concatenate.19), calls=%async_computation.2 | async-start | bytes 4194304 | tf_op jit(solution)/shard_map/all_to_all | solution.py:116
  177.6 50.4 %copy-start = (f32[1,2,16,128,128]{4,3,2,1,0:T(8,128)S(1)}, f32[1,2,16,128,128]{4,3,2,1,0:T(8,128)}, u32[]{:S(2)}) copy-start(f32[1,2,16,128,128]{4,3,2,1,0:T(8,128)} %get-tuple-element.13) | copy-start | bytes 6291460
  225.4 13.2 %slice-start = ((s8[8388608]{0:T(1024)(128)(4,1)}), s8[4194304]{0:T(1024)(128)(4,1)S(1)}, s32[]{:S(2)}) async-start(s8[8388608]{0:T(1024)(128)(4,1)} %bitcast.81), calls=%async_computation.3 | async-start | bytes 8388608
  228.0 10.5 %slice-start.1 = ((s8[8388608]{0:T(1024)(128)(4,1)}), s8[4194304]{0:T(1024)(128)(4,1)S(1)}, s32[]{:S(2)}) async-start(s8[8388608]{0:T(1024)(128)(4,1)} %bitcast.81), calls=%async_computation.4 | async-start | bytes 8388608
  228.0 10.5 %copy-start.3 = (f32[4,256,32]{1,2,0:T(8,128)S(1)}, f32[4,256,32]{1,2,0:T(8,128)}, u32[]{:S(2)}) copy-start(f32[4,256,32]{1,2,0:T(8,128)} %get-tuple-element.26) | copy-start | bytes 393220
  228.1 10.5 %copy-start.4 = (pred[256,256]{1,0:T(8,128)(4,1)S(1)}, pred[256,256]{1,0:T(8,128)(4,1)}, u32[]{:S(2)}) copy-start(pred[256,256]{1,0:T(8,128)(4,1)} %iota_compare_fusion) | copy-start | bytes 196612
  294.2 16.4 %copy-start.5 = (f32[4096]{0:T(1024)S(1)}, f32[4096]{0:T(1024)}, u32[]{:S(2)}) copy-start(f32[4096]{0:T(1024)} %param.21) | copy-start | bytes 49156
where the time goes:
time: 328 us; the launch traced here: 325 us
  local copies, waits for them, and re-layouts  94.1 us (29%)
  waiting for transfers between devices  85.5 us (26%)
  other arithmetic  79.9 us (24%)
  matrix products  35.5 us (11%)
  starting transfers between devices  23.5 us (7%)
  blocking collectives  5.67 us (2%)
    all_to_all x1, waiting for transfers between devices, local(): lax.all_to_all(flat_states, 'seq', split_axis=0, concat_axis=0, tiled=True)  45.2 us
    all_to_all x1, waiting for transfers between devices, local(): lax.all_to_all(ordered, 'seq', split_axis=0, concat_axis=0, tiled=True)  40.2 us
    add x1, local copies, waits for them, and re-layouts, local(): local_part + carried_part + skip_part  19.9 us
    unnamed x40, local copies, waits for them, and re-layouts  19.6 us
    unnamed x2, other arithmetic  18.9 us
    reshape x1, local copies, waits for them, and re-layouts, local(): (local_part + carried_part + skip_part).reshape(row_count, channels)  18.2 us
    dot_general x1, matrix products, local(): jnp.einsum('cghls,csghp->clghp', mixing, x_heads, preferred_element_type=...  17.5 us
    convert_element_type x1, other arithmetic, local(): return (gated_out * inverse_rms[:, None] * norm_gain).astype(jnp.bfloat16)  13.9 us
  transfers between devices with their start and end apart: 5, of which 2 were waited for; matrix products, arithmetic and copies ran while one was open for 27% of the time, Pallas kernels for 0%

commit v1 on v0

--- a/solution.py
+++ b/solution.py
@@ -6,6 +6,28 @@
 SPAN = 256
 INNER = 16384
 norm_eps = 1e-05
+
+
+def in_blocks(x, dim, size):
+    before, after = (x.shape[:dim], x.shape[dim + 1 :])
+    return jnp.moveaxis(x.reshape(*before, size, -1, *after), dim, 0)
+
+
+def joined_along(blocks, dim):
+    dims = list(blocks.shape[1:])
+    dims[dim] *= blocks.shape[0]
+    return jnp.moveaxis(blocks, 0, dim).reshape(dims)
+
+
+def exchange_in_pairs(shard, axis, split_dim, concat_dim):
+    size, index = (lax.axis_size(axis), lax.axis_index(axis))
+    blocks = in_blocks(shard, split_dim, size)
+    gathered = [blocks[index]]
+    for turn in range(1, size):
+        sent = blocks[index ^ turn]
+        gathered.append(lax.ppermute(sent, axis, [(i, i ^ turn) for i in range(size)]))
+    blocks = jnp.stack(gathered)[index ^ jnp.arange(size)]
+    return joined_along(blocks, concat_dim)
 
 
 def from_behind(value, axis, by):
@@ -110,7 +132,7 @@
     ordered = prefix_sources(
         (
             lax.all_to_all(piece_decays, "seq", split_axis=0, concat_axis=0, tiled=True),
-            lax.all_to_all(flat_states, "seq", split_axis=0, concat_axis=0, tiled=True),
+            exchange_in_pairs(flat_states, "seq", 0, 0),
         )
     )
     prefix = lax.all_to_all(ordered, "seq", split_axis=0, concat_axis=0, tiled=True).reshape(

time: 328 us -> 333 us (1.015)
  waiting for transfers between devices: 85.5 us -> 66.7 us
  starting transfers between devices: 23.5 us -> 37.4 us
  local copies, waits for them, and re-layouts: 94.1 us -> 107 us
    all_to_all x1 -> x0, waiting for transfers between devices: 45.2 us -> none  [local(): lax.all_to_all(flat_states, 'seq', split_axis=0, concat_axis=0, tiled=True)]
    ppermute x0 -> x7, waiting for transfers between devices: none -> 28.8 us  [exchange_in_pairs(): lax.ppermute(sent, axis, [(i, i ^ turn) for i in range(size)])]
    ppermute x0 -> x7, starting transfers between devices: none -> 12.5 us  [exchange_in_pairs(): lax.ppermute(sent, axis, [(i, i ^ turn) for i in range(size)])]
    all_to_all x1, starting transfers between devices: 4.38 us -> 11.8 us  [local(): lax.all_to_all(ordered, 'seq', split_axis=0, concat_axis=0, tiled=True)]
    slice x1, local copies, waits for them, and re-layouts: 0.26 us -> 6.27 us  [prefix_sources(): inclusive[1][:-1]]
    all_to_all x1 -> x0, starting transfers between devices: 5.98 us -> none  [local(): lax.all_to_all(flat_states, 'seq', split_axis=0, concat_axis=0, tiled=True)]
    unnamed x40 -> x62, local copies, waits for them, and re-layouts: 19.6 us -> 24.5 us
  transfers between devices with their start and end apart: 5 -> 11, of which waited for: 2 -> 3; matrix products, arithmetic and copies ran while one was open for 27% -> 26% of each run, Pallas kernels for 0% -> 0%
where the time goes in v1:
time: 333 us; the launch traced here: 330 us
  local copies, waits for them, and re-layouts  107 us (32%)
  other arithmetic  77.2 us (23%)
  waiting for transfers between devices  66.7 us (20%)
  starting transfers between devices  37.4 us (11%)
  matrix products  35.6 us (11%)
  blocking collectives  5.67 us (2%)
    all_to_all x1, waiting for transfers between devices, local(): lax.all_to_all(ordered, 'seq', split_axis=0, concat_axis=0, tiled=True)  37.9 us
    ppermute x7, waiting for transfers between devices, exchange_in_pairs(): lax.ppermute(sent, axis, [(i, i ^ turn) for i in range(size)])  28.8 us
    unnamed x62, local copies, waits for them, and re-layouts  24.5 us
    add x1, local copies, waits for them, and re-layouts, local(): local_part + carried_part + skip_part  19.9 us
    unnamed x2, other arithmetic  18.9 us
    reshape x1, local copies, waits for them, and re-layouts, local(): (local_part + carried_part + skip_part).reshape(row_count, channels)  18.2 us
    dot_general x1, matrix products, local(): jnp.einsum('cghls,csghp->clghp', mixing, x_heads, preferred_element_type=...  17.5 us
    convert_element_type x1, other arithmetic, local(): return (gated_out * inverse_rms[:, None] * norm_gain).astype(jnp.bfloat16)  13.9 us
  transfers between devices with their start and end apart: 11, of which 3 were waited for; matrix products, arithmetic and copies ran while one was open for 26% of the time, Pallas kernels for 0%

profile of v1, /device:TPU:0, one launch (start us, length us, event | category | flops | bytes accessed | tf_op | source)
XLA Modules:
  0.0 330.3 jit_solution(5911822677085195959)
XLA Ops:
  0.8 4.9 %collective-permute-start.1 = (bf16[2,3,256]{2,1,0:T(4,128)(2,1)S(1)}, bf16[2,3,256]{2,1,0:T(4,128)(2,1)S(1)}, u32[]{:S(2)}, u32[]{:S(2)}) collective-permute-start(bf16[2,3,256]{2,1,0:T(4,128)(2,1)S(1)} %slice.176), channel_id=1, source_target_pairs={{0,1},{1,2},{2,3},{3,4},{4,5},{5,6},{6,7},{8,9},{9,10},{10,11},{11... | collective-permute-start | bytes 9224 | tf_op jit(solution)/shard_map/ppermute | solution.py:36
  6.5 3.4 %collective-permute-start = (bf16[3,4096]{1,0:T(4,128)(2,1)S(1)}, bf16[3,4096]{1,0:T(4,128)(2,1)S(1)}, u32[]{:S(2)}, u32[]{:S(2)}) collective-permute-start(bf16[3,4096]{1,0:T(4,128)(2,1)S(1)} %slice.168), channel_id=1, source_target_pairs={{0,1},{1,2},{2,3},{3,4},{4,5},{5,6},{6,7},{8,9},{9,10},{10,11},{11... | collective-permute-start | bytes 73736 | tf_op jit(solution)/shard_map/ppermute | solution.py:36
  12.0 2.3 reduce-window.6
  16.0 4.8 %all-to-all-start = ((f32[8,1,4]{2,1,0:T(1,128)}), f32[8,1,4]{2,1,0:T(1,128)}, u32[]{:S(2)}, u32[]{:S(2)}) async-start(f32[8,1,4]{2,1,0:T(1,128)} %bitcast.34), calls=%async_computation | async-start | bytes 8192 | tf_op jit(solution)/shard_map/all_to_all | solution.py:134
  27.5 18.9 %fusion.20 = bf16[128,8,32,128]{3,1,2,0:T(8,128)(2,1)} fusion(bf16[1024,4096]{1,0:T(8,128)(2,1)} %param.11, f32[4096]{0:T(1024)S(1)} %bitcast.131, bf16[3,4096]{1,0:T(4,128)(2,1)S(1)} %collective-permute-done, f32[4096]{0:T(1024)S(1)} %bitcast.132, f32[4096]{0:T(1024)S(1)} %bitcast.130, f32[4096]{0:T(1024)S(1)} %bitcast.129), kind=kLoop, calls=%fused_computation.33 | loop fusion | flops 104857600 | bytes 16867328
  46.5 9.4 %copy.115 = bf16[128,8,32,128]{3,2,1,0:T(8,128)(2,1)} copy(bf16[128,8,32,128]{3,1,2,0:T(8,128)(2,1)} %fusion.20) | data formatting | bytes 16777216
  55.9 13.7 %copy.89 = bf16[4,256,2,16,128]{1,4,3,2,0:T(8,128)(2,1)} copy(bf16[4,256,2,16,128]{4,3,2,1,0:T(8,128)(2,1)} %bitcast.114) | data formatting | bytes 16777216 | tf_op jit(solution)/shard_map/reshape | solution.py:104
  69.6 5.7 %fusion.16 = f32[4,2,16,128,128]{4,3,2,1,0:T(8,128)S(1)} fusion(bf16[4,256,2,16,128]{1,4,3,2,0:T(8,128)(2,1)} %copy.89, f32[4,256,2,16]{1,3,2,0:T(8,128)S(1)} %bitcast.127, bf16[4,256,2,128,1]{3,2,1,0,4:T(2,128)(2,1)S(1)} %bitcast.123), kind=kOutput, calls=%fused_computation.28 | convolution fusion | flops 1086324736 | bytes 17432576 | tf_op jit(solution)/shard_map/clghp,clgn->cghpn/dot_general | solution.py:112
  75.4 6.3 %multiply_add_fusion = (f32[1,2,16,128,128]{4,3,2,1,0:T(8,128)}, f32[1,2,16,128,128]{4,3,2,1,0:T(8,128)}, f32[1,2,16,128,128]{4,3,2,1,0:T(8,128)}, f32[1,2,16,12...) fusion(f32[2,16]{1,0:T(2,128)S(1)} %copy-done.20, ...), kind=kLoop, calls=%fused_computation.40 | loop fusion | flops 2621440 | bytes 23069056 | tf_op jit(solution)/shard_map/add | solution.py:123
  81.7 4.9 %select_add_fusion = f32[8,1,4,128,128]{4,3,2,0,1:T(8,128)S(1)} fusion(f32[8,1,4,128,128]{4,3,2,0,1:T(8,128)} %bitcast.121, f32[8,1,4,128,128]{4,3,2,0,1:T(8,128)} %bitcast.120, f32[8,1,4,128,128]{4,3,2,0,1:T(8,128)} %bitcast.119, f32[8,1,4,128,128]{4,3,2,0,1:T(8,128)} %bitcast.118, f32[8,1,4,128,128]{4,3,2,0,1:T(8,128)} %bitcast.117, ...), kind=kLoop, calls=%fused_computation.39 | loop fusion | flops 5242880 | bytes 12583553 | tf_op jit(solution)/shard_map/add | solution.py:127
  87.7 2.0 collective-permute-start.2
  93.2 2.9 collective-permute-start.5
  97.5 3.3 collective-permute-start.7
  101.8 8.6 %collective-permute-done.3 = f32[1,4,128,128]{3,2,1,0:T(8,128)} collective-permute-done((f32[1,4,128,128]{3,2,1,0:T(8,128)}, f32[1,4,128,128]{3,2,1,0:T(8,128)}, u32[]{:S(2)}, u32[]{:S(2)}) %collective-permute-start.3) | collective-permute-done | bytes 262176 | tf_op jit(solution)/shard_map/ppermute | solution.py:28
  112.6 20.2 %collective-permute-done.6 = f32[1,4,128,128]{3,2,1,0:T(8,128)S(1)} collective-permute-done((f32[1,4,128,128]{3,2,1,0:T(8,128)S(1)}, f32[1,4,128,128]{3,2,1,0:T(8,128)S(1)}, u32[]{:S(2)}, u32[]{:S(2)}) %collective-permute-start.6) | collective-permute-done | bytes 262176 | tf_op jit(solution)/shard_map/ppermute | solution.py:28
  134.3 2.3 gather_fusion
  139.4 3.5 %pad.22 = f32[4,4,128,128]{3,2,1,0:T(8,128)S(1)} pad(f32[2,4,128,128]{3,2,1,0:T(8,128)} %pad_maximum_fusion.3, f32[]{:T(128)} %constant.15.clone.1), padding=0_1_1x0_0_0x0_0_0x0_0_0 | pad | bytes 1572868 | tf_op jit(solution)/shard_map/pad | solution.py:44
  142.9 5.7 %pad.23 = f32[4,4,128,128]{3,2,1,0:T(8,128)} pad(f32[2,4,128,128]{3,2,1,0:T(8,128)} %pad_add_fusion, f32[]{:T(128)} %constant.15.clone.1), padding=1_0_1x0_0_0x0_0_0x0_0_0 | pad | bytes 1572868 | tf_op jit(solution)/shard_map/pad | solution.py:44
  148.6 2.3 add.232
  151.0 10.1 %pad.116 = f32[8,4,128,128]{3,2,1,0:T(8,128)} pad(f32[4,4,128,128]{3,2,1,0:T(8,128)} %add.232, f32[]{:T(128)} %constant.15.clone.1), padding=1_0_1x0_0_0x0_0_0x0_0_0 | pad | bytes 3145732
  162.5 6.3 %pad.48 = f32[7,4,128,128]{3,2,1,0:T(8,128)} pad(f32[4,4,128,128]{3,2,1,0:T(8,128)S(1)} %pad_maximum_fusion.2, f32[]{:T(128)} %constant.15.clone.1), padding=0_0_1x0_0_0x0_0_0x0_0_0 | pad | bytes 2883588 | tf_op jit(solution)/shard_map/slice | solution.py:45
  172.2 11.8 %all-to-all-start.1 = ((f32[8,4,128,128]{3,2,1,0:T(8,128)}), f32[8,4,128,128]{3,2,1,0:T(8,128)S(1)}, u32[]{:S(2)}, u32[]{:S(2)}) async-start(f32[8,4,128,128]{3,2,1,0:T(8,128)} %concatenate.19), calls=%async_computation.1 | async-start | bytes 4194304 | tf_op jit(solution)/shard_map/all_to_all | solution.py:138
  185.4 3.2 broadcast_select_fusion
  191.6 37.9 %all-to-all-done.1 = f32[8,4,128,128]{3,2,1,0:T(8,128)S(1)} async-done(((f32[8,4,128,128]{3,2,1,0:T(8,128)}), f32[8,4,128,128]{3,2,1,0:T(8,128)S(1)}, u32[]{:S(2)}, u32[]{:S(2)}) %all-to-all-start.1) | async-done | bytes 2097184 | tf_op jit(solution)/shard_map/all_to_all | solution.py:138
  230.8 2.6 bitcast_add_fusion
  233.7 10.6 %fusion.21 = f32[4,2,16,128,256]{4,3,2,1,0:T(8,128)} fusion(f32[1,2,16,128,128]{4,3,2,1,0:T(8,128)S(1)} %copy-done, f32[1,2,16,128,128]{4,3,2,1,0:T(8,128)} %get-tuple-element.14, f32[1,2,16,128,128]{4,3,2,1,0:T(8,128)} %get-tuple-element.15, f32[4]{0:T(128)S(1)} %pad.35.clone, f32[2,16,128,128]{3,2,1,0:T(8,128)S(1)} %bitcast_add_fusion, ...), kind=kOutput, calls=%fused_computation.34 | convolution fusion | flops 1086324736 | bytes 25690640 | tf_op jit(solution)/shard_map/clgn,cghpn->clghp/dot_general | solution.py:146
  244.3 17.5 %fusion.2 = f32[4,256,2,16,128]{1,4,3,2,0:T(8,128)} fusion(bf16[4,256,2,16,128]{1,4,3,2,0:T(8,128)(2,1)S(1)} %bitcast.113, f32[4,2,16,128,256]{4,3,2,1,0:T(8,128)} %fusion.21, f32[4,2,16,256]{3,2,1,0:T(8,128)S(1)} %copy.88, f32[4,2,16,256]{3,2,1,0:T(8,128)S(1)} %reduce_window_sum.27, f32[4,2,256,256]{3,2,1,0:T(8,128)} %fusion.31, ...), kind=kOutput, calls=%fused_computation.8 | convolution fusion | flops 2218786816 | bytes 44499072 | tf_op jit(solution)/shard_map/cghls,csghp->clghp/dot_general | solution.py:105
  261.8 19.9 %copy.100 = f32[4,256,2,16,128]{4,3,2,1,0:T(8,128)} copy(f32[4,256,2,16,128]{1,4,3,2,0:T(8,128)} %fusion.2) | data formatting | bytes 33554432 | tf_op jit(solution)/shard_map/add | solution.py:148
  281.7 18.2 %reshape.320 = f32[1024,4096]{1,0:T(8,128)} reshape(f32[4,256,2,16,128]{4,3,2,1,0:T(8,128)} %copy.100) | data formatting | bytes 33554432 | tf_op jit(solution)/shard_map/reshape | solution.py:148
  299.9 10.7 %multiply_reduce_fusion = f32[1024]{0:T(1024)S(1)} fusion(f32[1024,4096]{1,0:T(8,128)} %reshape.320, bf16[1024,4096]{1,0:T(8,128)(2,1)} %param.14), kind=kLoop, calls=%fused_computation.16 | loop fusion | flops 33553408 | bytes 25169920 | tf_op jit(solution)/shard_map/reduce_sum | solution.py:150
  310.7 5.7 %psum.7 = f32[1024]{0:T(1024)S(1)} all-reduce(f32[1024]{0:T(1024)S(1)} %multiply_reduce_fusion), channel_id=1, replica_groups=mesh['head'=4,'seq'=8] {'head'}, use_global_device_ids=true, to_apply=%region_3.4 | all-reduce | flops 1024 | bytes 8192 | tf_op jit(solution)/shard_map/psum | solution.py:151
  316.4 13.9 %multiply_convert_fusion.2 = bf16[1024,4096]{1,0:T(8,128)(2,1)} fusion(f32[4096]{0:T(1024)S(1)} %copy-done.11, f32[1024]{0:T(1024)S(1)} %add_rsqrt_fusion, f32[1024,4096]{1,0:T(8,128)} %reshape.320, bf16[1024,4096]{1,0:T(8,128)(2,1)} %param.14), kind=kLoop, calls=%fused_computation.15 | loop fusion | flops 37748736 | bytes 33574912 | tf_op jit(solution)/shard_map/convert_element_type | solution.py:153
  (149 shorter events, 36.0 us)
Async XLA Ops:
  0.0 25.0 %copy-start.6 = (bf16[2,1024,256]{2,1,0:T(8,128)(2,1)S(1)}, bf16[2,1024,256]{2,1,0:T(8,128)(2,1)}, u32[]{:S(2)}) copy-start(bf16[2,1024,256]{2,1,0:T(8,128)(2,1)} %param.12) | copy-start | bytes 3145732
  0.0 20.8 %copy-start.13 = (f32[2,4,256]{2,1,0:T(4,128)S(1)}, f32[2,4,256]{2,1,0:T(4,128)}, u32[]{:S(2)}) copy-start(f32[2,4,256]{2,1,0:T(4,128)} %param.16) | copy-start | bytes 24580
  0.0 21.6 %copy-start.9 = (f32[4,4096]{1,0:T(4,128)S(1)}, f32[4,4096]{1,0:T(4,128)}, u32[]{:S(2)}) copy-start(f32[4,4096]{1,0:T(4,128)} %param.15) | copy-start | bytes 196612
  0.8 24.2 %collective-permute-start.1 = (bf16[2,3,256]{2,1,0:T(4,128)(2,1)S(1)}, bf16[2,3,256]{2,1,0:T(4,128)(2,1)S(1)}, u32[]{:S(2)}, u32[]{:S(2)}) collective-permute-start(bf16[2,3,256]{2,1,0:T(4,128)(2,1)S(1)} %slice.176), channel_id=1, source_target_pairs={{0,1},{1,2},{2,3},{3,4},{4,5},{5,6},{6,7},{8,9},{9,10},{10,11},{11... | collective-permute-start | bytes 9224 | tf_op jit(solution)/shard_map/ppermute | solution.py:36
  6.5 21.0 %collective-permute-start = (bf16[3,4096]{1,0:T(4,128)(2,1)S(1)}, bf16[3,4096]{1,0:T(4,128)(2,1)S(1)}, u32[]{:S(2)}, u32[]{:S(2)}) collective-permute-start(bf16[3,4096]{1,0:T(4,128)(2,1)S(1)} %slice.168), channel_id=1, source_target_pairs={{0,1},{1,2},{2,3},{3,4},{4,5},{5,6},{6,7},{8,9},{9,10},{10,11},{11... | collective-permute-start | bytes 73736 | tf_op jit(solution)/shard_map/ppermute | solution.py:36
  15.3 12.1 %copy-start.14 = (f32[32]{0:T(128)}, f32[32]{0:T(128)S(1)}, u32[]{:S(2)}) copy-start(f32[32]{0:T(128)S(1)} %get-tuple-element.48) | copy-start | bytes 388
  15.3 12.1 %copy-start.16 = (f32[32]{0:T(128)}, f32[32]{0:T(128)S(1)}, u32[]{:S(2)}) copy-start(f32[32]{0:T(128)S(1)} %get-tuple-element.46) | copy-start | bytes 388
  16.0 73.7 %all-to-all-start = ((f32[8,1,4]{2,1,0:T(1,128)}), f32[8,1,4]{2,1,0:T(1,128)}, u32[]{:S(2)}, u32[]{:S(2)}) async-start(f32[8,1,4]{2,1,0:T(1,128)} %bitcast.34), calls=%async_computation | async-start | bytes 8192 | tf_op jit(solution)/shard_map/all_to_all | solution.py:134
  27.5 42.1 %copy-start.3 = (bf16[4,256,2,128]{3,2,1,0:T(2,128)(2,1)}, bf16[4,256,2,128]{3,2,1,0:T(2,128)(2,1)S(1)}, u32[]{:S(2)}) copy-start(bf16[4,256,2,128]{3,2,1,0:T(2,128)(2,1)S(1)} %reshape_squeeze.7) | copy-start | bytes 1572868
  69.6 5.8 %copy-start.18 = (f32[2,16]{1,0:T(2,128)S(1)}, f32[2,16]{1,0:T(2,128)}, u32[]{:S(2)}) copy-start(f32[2,16]{1,0:T(2,128)} %mul.450) | copy-start | bytes 388
  69.6 5.8 %copy-start.19 = (f32[2,16]{1,0:T(2,128)S(1)}, f32[2,16]{1,0:T(2,128)}, u32[]{:S(2)}) copy-start(f32[2,16]{1,0:T(2,128)} %mul.456) | copy-start | bytes 388
  69.6 5.8 %copy-start.20 = (f32[2,16]{1,0:T(2,128)S(1)}, f32[2,16]{1,0:T(2,128)}, u32[]{:S(2)}) copy-start(f32[2,16]{1,0:T(2,128)} %mul.459) | copy-start | bytes 388
  75.4 6.4 %copy-start.12 = (f32[8,4]{1,0:T(8,128)S(1)}, f32[8,4]{1,0:T(8,128)}, u32[]{:S(2)}) copy-start(f32[8,4]{1,0:T(8,128)} %get-tuple-element.45) | copy-start | bytes 388
  87.7 9.8 %collective-permute-start.2 = (f32[1,4,128,128]{3,2,1,0:T(8,128)}, f32[1,4,128,128]{3,2,1,0:T(8,128)}, u32[]{:S(2)}, u32[]{:S(2)}) collective-permute-start(f32[1,4,128,128]{3,2,1,0:T(8,128)} %get-tuple-element.26), channel_id=1, source_target_pairs={{0,1},{1,0},{2,3},{3,2},{4,5},{5,4},{6,7},{7,6},{8,9},{9,8},{10,11... | collective-permute-start | bytes 786440 | tf_op jit(solution)/shard_map/ppermute | solution.py:28
  91.1 19.3 %collective-permute-start.3 = (f32[1,4,128,128]{3,2,1,0:T(8,128)}, f32[1,4,128,128]{3,2,1,0:T(8,128)}, u32[]{:S(2)}, u32[]{:S(2)}) collective-permute-start(f32[1,4,128,128]{3,2,1,0:T(8,128)} %get-tuple-element.25), channel_id=1, source_target_pairs={{0,2},{1,3},{2,0},{3,1},{4,6},{5,7},{6,4},{7,5},{8,10},{9,11},{10,... | collective-permute-start | bytes 786440 | tf_op jit(solution)/shard_map/ppermute | solution.py:28
  93.2 19.4 %collective-permute-start.4 = (f32[1,4,128,128]{3,2,1,0:T(8,128)}, f32[1,4,128,128]{3,2,1,0:T(8,128)S(1)}, u32[]{:S(2)}, u32[]{:S(2)}) collective-permute-start(f32[1,4,128,128]{3,2,1,0:T(8,128)} %get-tuple-element.24), channel_id=1, source_target_pairs={{0,3},{1,2},{2,1},{3,0},{4,7},{5,6},{6,5},{7,4},{8,11},{9,10},{10,... | collective-permute-start | bytes 786440 | tf_op jit(solution)/shard_map/ppermute | solution.py:28
  93.2 19.4 %collective-permute-start.5 = (f32[1,4,128,128]{3,2,1,0:T(8,128)S(1)}, f32[1,4,128,128]{3,2,1,0:T(8,128)S(1)}, u32[]{:S(2)}, u32[]{:S(2)}) collective-permute-start(f32[1,4,128,128]{3,2,1,0:T(8,128)S(1)} %get-tuple-element.23), channel_id=1, source_target_pairs={{0,4},{1,5},{2,6},{3,7},{4,0},{5,1},{6,2},{7,3},{8,12},{9,13},{10,... | collective-permute-start | bytes 786440 | tf_op jit(solution)/shard_map/ppermute | solution.py:28
  96.1 36.8 %collective-permute-start.6 = (f32[1,4,128,128]{3,2,1,0:T(8,128)S(1)}, f32[1,4,128,128]{3,2,1,0:T(8,128)S(1)}, u32[]{:S(2)}, u32[]{:S(2)}) collective-permute-start(f32[1,4,128,128]{3,2,1,0:T(8,128)S(1)} %get-tuple-element.22), channel_id=1, source_target_pairs={{0,5},{1,4},{2,7},{3,6},{4,1},{5,0},{6,3},{7,2},{8,13},{9,12},{10,... | collective-permute-start | bytes 786440 | tf_op jit(solution)/shard_map/ppermute | solution.py:28
  97.5 35.3 %collective-permute-start.7 = (f32[1,4,128,128]{3,2,1,0:T(8,128)S(1)}, f32[1,4,128,128]{3,2,1,0:T(8,128)S(1)}, u32[]{:S(2)}, u32[]{:S(2)}) collective-permute-start(f32[1,4,128,128]{3,2,1,0:T(8,128)S(1)} %get-tuple-element.21), channel_id=1, source_target_pairs={{0,6},{1,7},{2,4},{3,5},{4,2},{5,3},{6,0},{7,1},{8,14},{9,15},{10,... | collective-permute-start | bytes 786440 | tf_op jit(solution)/shard_map/ppermute | solution.py:28
  110.3 22.6 %collective-permute-start.8 = (f32[1,4,128,128]{3,2,1,0:T(8,128)S(1)}, f32[1,4,128,128]{3,2,1,0:T(8,128)S(1)}, u32[]{:S(2)}, u32[]{:S(2)}) collective-permute-start(f32[1,4,128,128]{3,2,1,0:T(8,128)S(1)} %get-tuple-element.20), channel_id=1, source_target_pairs={{0,7},{1,6},{2,5},{3,4},{4,3},{5,2},{6,1},{7,0},{8,15},{9,14},{10,... | collective-permute-start | bytes 786440 | tf_op jit(solution)/shard_map/ppermute | solution.py:28
  162.4 6.4 %copy-start.2 = (f32[8,4,128,128]{3,2,1,0:T(8,128)S(1)}, f32[8,4,128,128]{3,2,1,0:T(8,128)}, u32[]{:S(2)}) copy-start(f32[8,4,128,128]{3,2,1,0:T(8,128)} %pad.116) | copy-start | bytes 6291460
  172.1 11.9 %copy-start.17 = (f32[32]{0:T(128)S(1)}, f32[32]{0:T(128)}, u32[]{:S(2)}) copy-start(f32[32]{0:T(128)} %copy-done.16) | copy-start | bytes 388
  172.1 11.9 %copy-start.15 = (f32[32]{0:T(128)S(1)}, f32[32]{0:T(128)}, u32[]{:S(2)}) copy-start(f32[32]{0:T(128)} %copy-done.14) | copy-start | bytes 388
  172.1 12.0 %copy-start.22 = (f32[32]{0:T(128)S(1)}, f32[32]{0:T(128)}, u32[]{:S(2)}) copy-start(f32[32]{0:T(128)} %get-tuple-element.5) | copy-start | bytes 388
  172.1 12.5 %copy-start.23 = (f32[32]{0:T(128)S(1)}, f32[32]{0:T(128)}, u32[]{:S(2)}) copy-start(f32[32]{0:T(128)} %param.19) | copy-start | bytes 388
  172.2 57.4 %all-to-all-start.1 = ((f32[8,4,128,128]{3,2,1,0:T(8,128)}), f32[8,4,128,128]{3,2,1,0:T(8,128)S(1)}, u32[]{:S(2)}, u32[]{:S(2)}) async-start(f32[8,4,128,128]{3,2,1,0:T(8,128)} %concatenate.19), calls=%async_computation.1 | async-start | bytes 4194304 | tf_op jit(solution)/shard_map/all_to_all | solution.py:138
  185.4 4.4 %copy-start.4 = (bf16[4,256,2,128]{3,2,1,0:T(2,128)(2,1)S(1)}, bf16[4,256,2,128]{3,2,1,0:T(2,128)(2,1)}, u32[]{:S(2)}) copy-start(bf16[4,256,2,128]{3,2,1,0:T(2,128)(2,1)} %copy-done.3) | copy-start | bytes 1572868
  230.8 13.5 %slice-start = ((s8[8388608]{0:T(1024)(128)(4,1)}), s8[4194304]{0:T(1024)(128)(4,1)S(1)}, s32[]{:S(2)}) async-start(s8[8388608]{0:T(1024)(128)(4,1)} %bitcast.112), calls=%async_computation.2 | async-start | bytes 8388608
  233.7 10.6 %slice-start.1 = ((s8[8388608]{0:T(1024)(128)(4,1)}), s8[4194304]{0:T(1024)(128)(4,1)S(1)}, s32[]{:S(2)}) async-start(s8[8388608]{0:T(1024)(128)(4,1)} %bitcast.112), calls=%async_computation.3 | async-start | bytes 8388608
  233.7 10.6 %copy-start.8 = (f32[4,256,32]{1,2,0:T(8,128)S(1)}, f32[4,256,32]{1,2,0:T(8,128)}, u32[]{:S(2)}) copy-start(f32[4,256,32]{1,2,0:T(8,128)} %get-tuple-element.34) | copy-start | bytes 393220
  233.7 10.6 %copy-start.10 = (pred[256,256]{1,0:T(8,128)(4,1)S(1)}, pred[256,256]{1,0:T(8,128)(4,1)}, u32[]{:S(2)}) copy-start(pred[256,256]{1,0:T(8,128)(4,1)} %iota_compare_fusion) | copy-start | bytes 196612
  299.9 16.4 %copy-start.11 = (f32[4096]{0:T(1024)S(1)}, f32[4096]{0:T(1024)}, u32[]{:S(2)}) copy-start(f32[4096]{0:T(1024)} %param.21) | copy-start | bytes 49156
  (5 other events, 9.8 us)
